TPU v7x, 512 devices: a whole 4x4x16 slice. The times are simulated.
512 devices in a mesh: seq: 8 (over y, core), head: 64 (over z, x).
Axes of the slice: x: 4, y: 4, z: 16, core: 2. Of those that a mesh axis runs over, the one named last changes fastest.
Arguments:
- tokens: bfloat16 [8192, 2048], P('seq', 'head'), may hold values from -6 to 6
- z_weight: bfloat16 [2048, 4096], P(None, 'head'), may hold values from -0.125 to 0.125
- x_weight: bfloat16 [2048, 4096], P(None, 'head'), may hold values from -0.79549513 to 0.79549513
- bc_weight: bfloat16 [2048, 256], replicated, may hold values from -0.125 to 0.125
- step_weight: bfloat16 [2048, 64], P(None, 'head'), may hold values from -0.125 to 0.125
- x_kernel: float32 [4, 4096], P(None, 'head'), may hold values from -3 to 3
- bc_kernel: float32 [4, 256], replicated, may hold values from -3 to 3
- step_bias: float32 [64], P('head'), may hold values from -9 to -3
- log_decay: float32 [64], P('head'), may hold values from 0 to 1.5
- skip_gain: float32 [64], P('head'), may hold values from 0.2 to 0.8
- norm_gain: bfloat16 [4096], P('head'), may hold values from 0.099609375 to 1.8984375
- out_weight: bfloat16 [4096, 2048], P('head'), may hold values from -0.09375 to 0.09375
Outputs:
- mixed: bfloat16 [8192, 2048], P('seq', 'head')
All inputs are finite; a program needn't handle non-finite values.
Results may differ from a plain program's by a relative error of at most 0.017.
Values may be sent and summed in bfloat16 or wider, within the bound.
A program may use at most 64 MiB of HBM per device.

v0:
```python
import jax
import jax.numpy as jnp
from jax import lax
from jax.sharding import PartitionSpec as P

CH = 256


def from_behind(block, axis, distance):
    devices = range(lax.axis_size(axis))
    route = [(i - distance, i) for i in devices if i - distance in devices]
    return lax.ppermute(block, axis, route)


def causal(padded, kernel):
    length = padded.shape[0] - 3
    total = kernel[0] * padded[0:length].astype(jnp.float32)
    for offset in range(1, 4):
        total = total + kernel[offset] * padded[offset : offset + length].astype(jnp.float32)
    return jax.nn.silu(total).astype(jnp.bfloat16)


def body(
    tokens,
    z_weight,
    x_weight,
    bc_weight,
    step_weight,
    x_kernel,
    bc_kernel,
    step_bias,
    log_decay,
    skip_gain,
    norm_gain,
    out_weight,
):
    tok_rows = tokens.shape[0]
    heads_here = step_bias.shape[0]
    inner_width = x_weight.shape[1]
    head_size = inner_width // heads_here
    state_size = bc_weight.shape[1] // 2
    piece = lax.all_gather(tokens, "head", axis=1, tiled=True)

    def product(weight):
        return jnp.dot(piece, weight, preferred_element_type=jnp.float32)

    z_sum = product(z_weight)
    x_sum = product(x_weight)
    bc_sum = product(bc_weight)
    step_raw = product(step_weight)
    z_in = z_sum.astype(jnp.bfloat16)
    x_in = x_sum.astype(jnp.bfloat16)
    bc_in = bc_sum.astype(jnp.bfloat16)
    border = jnp.concatenate([x_in[-3:], bc_in[-3:]], axis=1)
    border = from_behind(border, "seq", 1)
    x_conv = causal(jnp.concatenate([border[:, :inner_width], x_in], axis=0), x_kernel)
    bc_conv = causal(jnp.concatenate([border[:, inner_width:], bc_in], axis=0), bc_kernel)
    blocks = tok_rows // CH
    b_map = bc_conv[:, :state_size].reshape(blocks, CH, state_size)
    c_map = bc_conv[:, state_size:].reshape(blocks, CH, state_size)
    step_size = jax.nn.softplus(step_raw + step_bias)
    rate = -jnp.exp(log_decay) * step_size
    values = x_conv.reshape(blocks, CH, heads_here, head_size)
    steps_b = step_size.reshape(blocks, CH, heads_here)
    cumulative = jnp.cumsum(rate.reshape(blocks, CH, heads_here), axis=1)
    lower = (jnp.arange(CH)[:, None] >= jnp.arange(CH)[None, :])[None, :, :, None]
    gram = jnp.einsum("ctn,csn->cts", c_map, b_map, preferred_element_type=jnp.float32)
    spread = cumulative[:, :, None, :] - cumulative[:, None, :, :]
    mixing = jnp.where(
        lower,
        gram[..., None] * jnp.exp(jnp.where(lower, spread, 0.0)) * steps_b[:, None, :, :],
        0.0,
    ).astype(jnp.bfloat16)
    intra = jnp.einsum("ctsh,cshp->cthp", mixing, values, preferred_element_type=jnp.float32)
    tails = jnp.exp(cumulative[:, -1:, :] - cumulative) * steps_b
    weighted = (values.astype(jnp.float32) * tails[..., None]).astype(jnp.bfloat16)
    local = jnp.einsum("cthp,ctn->chpn", weighted, b_map, preferred_element_type=jnp.float32)
    block_decay = jnp.exp(cumulative[:, -1, :])

    def advance(carry, item):
        state, decay = carry
        term, factor = item
        return ((factor[:, None, None] * state + term, decay * factor), (state, decay))

    zero_state = jnp.zeros((heads_here, head_size, state_size), jnp.float32)
    unit_decay = jnp.ones((heads_here,), jnp.float32)
    (shard_state, shard_decay), (local_in, decay_in) = lax.scan(
        advance, (zero_state, unit_decay), (local, block_decay)
    )

    def relay(index, carried):
        return from_behind(shard_decay[:, None, None] * carried + shard_state, "seq", 1)

    incoming = lax.fori_loop(0, lax.axis_size("seq") - 1, relay, zero_state)
    entering = local_in + decay_in[:, :, None, None] * incoming[None]
    held = entering.astype(jnp.bfloat16)
    from_state = (
        jnp.einsum("ctn,chpn->cthp", c_map, held, preferred_element_type=jnp.float32)
        * jnp.exp(cumulative)[..., None]
    )
    output_y = intra + from_state + skip_gain[None, None, :, None] * values.astype(jnp.float32)
    gated = (
        output_y.reshape(tok_rows, inner_width) * jax.nn.silu(z_in.astype(jnp.float32))
    ).astype(jnp.bfloat16)
    head_count = lax.axis_size("head")
    columns = lax.all_to_all(out_weight, "head", split_axis=1, concat_axis=0, tiled=True)
    gain_row = norm_gain.reshape(1, inner_width)
    section = lax.all_gather(gated, "head", axis=1, tiled=True)
    gain_part = lax.all_gather(gain_row, "head", axis=1, tiled=True)
    section_f = section.astype(jnp.float32)
    scaled = (section_f * gain_part.astype(jnp.float32)).astype(jnp.bfloat16)
    partial_out = jnp.dot(scaled, columns, preferred_element_type=jnp.float32)
    squares = jnp.sum(section_f * section_f, axis=1)
    meansq = squares / (inner_width * head_count)
    return (partial_out * lax.rsqrt(meansq + 1e-05)[:, None]).astype(jnp.bfloat16)


def solution(mesh):
    placed = (
        P("seq", "head"),
        P(None, "head"),
        P(None, "head"),
        P(),
        P(None, "head"),
        P(None, "head"),
        P(),
        P("head"),
        P("head"),
        P("head"),
        P("head"),
        P("head", None),
    )
    return jax.shard_map(
        body, mesh=mesh, in_specs=placed, out_specs=P("seq", "head"), check_vma=False
    )
```

profile of v0, /device:TPU:10, one launch (start us, length us, event | category | flops | bytes accessed | tf_op | source)
XLA Modules:
  0.0 403.9 jit_solution(2700277313001061849)
XLA Ops:
  11.0 148.9 %all-gather.4.cloned.1.call-done = bf16[1024,2048]{0,1:T(8,128)(2,1)} async-done(((bf16[1024,32]{0,1:T(8,128)(2,1)}), bf16[1024,2048]{0,1:T(8,128)(2,1)}) %all-gather.4.cloned.1.call-update) | async-done | bytes 4194320 | tf_op jit(solution)/shard_map/all_gather | solution.py:42
  160.0 2.8 fusion.45
  164.3 3.6 convolution_convert_fusion
  169.0 1.9 collective-permute-start.1
  171.3 3.5 collective-permute-done.1
  176.8 8.1 %while.28 = (s32[]{:T(128)}, f32[1,64,128]{2,1,0:T(8,128)S(1)}, f32[1]{0:T(128)}, f32[4,1,64,128]{3,2,1,0:T(8,128)S(1)}, f32[4,1]{0,1:T(1,128)S(1)}, /*index=5*/...) while((s32[]{:T(128)}, f32[1,64,128]{2,1,0:T(8,128)S(1)}, f32[1]{0:T(128)}, ...), condition=%wide.region_3.4_spmd.clone, body=%wide.region_2.3_spmd.clone.sunk | while | flops 32772 | bytes 164008 | solution.py:87
  185.4 36.8 %while.27 = (s32[]{:T(128)}, f32[1,64,128]{2,1,0:T(8,128)S(1)}, f32[1]{0:T(128)}, f32[1,64,128]{2,1,0:T(8,128)S(1)}, s32[]{:T(128)}) while((s32[]{:T(128)}, f32[1,64,128]{2,1,0:T(8,128)S(1)}, f32[1]{0:T(128)}, f32[1,64,128]{2,1,0:T(8,128)S(1)}, s32[]{:T(128)}) %tuple.53), condition=%wide.region_5.6_spmd, body=%wide.region_4.5_spmd.sunk | while | flops 16386 | bytes 229481 | solution.py:94
  185.4 2.1 collective-permute-start
  187.5 3.3 collective-permute-done
  190.8 1.9 collective-permute-start
  192.7 3.3 collective-permute-done
  196.0 1.9 collective-permute-start
  198.0 3.3 collective-permute-done
  203.2 3.3 collective-permute-done
  208.4 3.3 collective-permute-done
  211.7 1.9 collective-permute-start
  213.7 3.3 collective-permute-done
  217.0 1.9 collective-permute-start
  218.9 3.3 collective-permute-done
  222.7 3.7 multiply_convert_fusion.1
  227.8 10.3 %all-to-all-start = ((bf16[64,2,1024]{2,1,0:T(2,128)(2,1)}), bf16[64,2,1024]{2,1,0:T(2,128)(2,1)S(1)}, u32[]{:S(2)}, u32[]{:S(2)}) async-start(bf16[64,2,1024]{2,1,0:T(2,128)(2,1)} %reshape.305), calls=%async_computation | async-start | bytes 524288 | tf_op jit(solution)/shard_map/all_to_all | solution.py:106
  240.3 147.3 %all-reduce = bf16[4096]{0:T(1024)(128)(2,1)S(1)} all-reduce(bf16[4096]{0:T(1024)(128)(2,1)S(1)} %dynamic-update-slice), channel_id=2, replica_groups=mesh['seq'=8,'head'=64] {'head'}, use_global_device_ids=true, to_apply=%add | all-reduce | flops 4096 | bytes 16384
  388.7 5.2 %fusion.1 = f32[1024]{0:T(1024)S(1)} fusion(bf16[1024,4096]{0,1:T(8,128)(2,1)} %all-gather.6.cloned.1.call-done), kind=kLoop, calls=%fused_computation.7 | loop fusion | flops 12581888 | bytes 8392704 | tf_op jit(solution)/shard_map/reduce_sum | solution.py:113
  394.5 2.5 fusion.17
  (93 shorter events, 22.0 us)
Async XLA Ops:
  6.5 157.7 %copy-start = (bf16[2048,256]{1,0:T(8,128)(2,1)S(1)}, bf16[2048,256]{1,0:T(8,128)(2,1)}, u32[]{:S(2)}) copy-start(bf16[2048,256]{1,0:T(8,128)(2,1)} %param.19) | copy-start | bytes 3145732
  6.5 153.4 %all-gather.4.cloned.1.call-start = ((), (), s32[]{:S(2)}) async-start(), calls=%async_computation.1 | async-start | bytes 4259840 | tf_op jit(solution)/shard_map/all_gather | solution.py:42
  7.3 381.4 %all-gather.6.cloned.1.call-start = ((), (), s32[]{:S(2)}) async-start(), calls=%async_computation.2 | async-start | bytes 8519680 | tf_op jit(solution)/shard_map/all_gather | solution.py:108
  164.3 3.8 copy-start.1
  164.3 3.8 copy-start.3
  169.0 5.8 %collective-permute-start.1 = (bf16[3,320]{0,1:T(8,128)(2,1)S(1)}, bf16[3,320]{0,1:T(8,128)(2,1)S(1)}, u32[]{:S(2)}, u32[]{:S(2)}) collective-permute-start(bf16[3,320]{0,1:T(8,128)(2,1)S(1)} %pad_maximum_fusion.2), channel_id=1, source_target_pairs={{0,64},{64,128},{128,192},{192,256},{256,320},{320,384},{384,448},... | collective-permute-start | bytes 5768 | tf_op jit(solution)/shard_map/ppermute | solution.py:12
  176.2 46.5 %copy-start.4 = (bf16[2048,64]{0,1:T(8,128)(2,1)S(1)}, bf16[2048,64]{0,1:T(8,128)(2,1)}, u32[]{:S(2)}) copy-start(bf16[2048,64]{0,1:T(8,128)(2,1)} %param.17) | copy-start | bytes 786436
  185.4 41.1 %copy-start.5 = (bf16[64,2048]{1,0:T(8,128)(2,1)S(1)}, bf16[64,2048]{1,0:T(8,128)(2,1)}, u32[]{:S(2)}) copy-start(bf16[64,2048]{1,0:T(8,128)(2,1)} %param.27) | copy-start | bytes 786436
  185.4 5.4 %collective-permute-start = (f32[1,64,128]{2,1,0:T(8,128)S(1)}, f32[1,64,128]{2,1,0:T(8,128)S(1)}, u32[]{:S(2)}, u32[]{:S(2)}) collective-permute-start(f32[1,64,128]{2,1,0:T(8,128)S(1)} %multiply_add_fusion.2), channel_id=1, source_target_pairs={{0,64},{64,128},{128,192},{192,256},{256,320},{320,384},{384,448},... | collective-permute-start | bytes 98312 | tf_op jit(solution)/shard_map/while/body/eval_jaxpr/ppermute | solution.py:12
  190.8 5.2 %collective-permute-start = (f32[1,64,128]{2,1,0:T(8,128)S(1)}, f32[1,64,128]{2,1,0:T(8,128)S(1)}, u32[]{:S(2)}, u32[]{:S(2)}) collective-permute-start(f32[1,64,128]{2,1,0:T(8,128)S(1)} %multiply_add_fusion.2), channel_id=1, source_target_pairs={{0,64},{64,128},{128,192},{192,256},{256,320},{320,384},{384,448},... | collective-permute-start | bytes 98312 | tf_op jit(solution)/shard_map/while/body/eval_jaxpr/ppermute | solution.py:12
  196.0 5.2 %collective-permute-start = (f32[1,64,128]{2,1,0:T(8,128)S(1)}, f32[1,64,128]{2,1,0:T(8,128)S(1)}, u32[]{:S(2)}, u32[]{:S(2)}) collective-permute-start(f32[1,64,128]{2,1,0:T(8,128)S(1)} %multiply_add_fusion.2), channel_id=1, source_target_pairs={{0,64},{64,128},{128,192},{192,256},{256,320},{320,384},{384,448},... | collective-permute-start | bytes 98312 | tf_op jit(solution)/shard_map/while/body/eval_jaxpr/ppermute | solution.py:12
  201.3 5.2 %collective-permute-start = (f32[1,64,128]{2,1,0:T(8,128)S(1)}, f32[1,64,128]{2,1,0:T(8,128)S(1)}, u32[]{:S(2)}, u32[]{:S(2)}) collective-permute-start(f32[1,64,128]{2,1,0:T(8,128)S(1)} %multiply_add_fusion.2), channel_id=1, source_target_pairs={{0,64},{64,128},{128,192},{192,256},{256,320},{320,384},{384,448},... | collective-permute-start | bytes 98312 | tf_op jit(solution)/shard_map/while/body/eval_jaxpr/ppermute | solution.py:12
  206.5 5.2 %collective-permute-start = (f32[1,64,128]{2,1,0:T(8,128)S(1)}, f32[1,64,128]{2,1,0:T(8,128)S(1)}, u32[]{:S(2)}, u32[]{:S(2)}) collective-permute-start(f32[1,64,128]{2,1,0:T(8,128)S(1)} %multiply_add_fusion.2), channel_id=1, source_target_pairs={{0,64},{64,128},{128,192},{192,256},{256,320},{320,384},{384,448},... | collective-permute-start | bytes 98312 | tf_op jit(solution)/shard_map/while/body/eval_jaxpr/ppermute | solution.py:12
  211.7 5.2 %collective-permute-start = (f32[1,64,128]{2,1,0:T(8,128)S(1)}, f32[1,64,128]{2,1,0:T(8,128)S(1)}, u32[]{:S(2)}, u32[]{:S(2)}) collective-permute-start(f32[1,64,128]{2,1,0:T(8,128)S(1)} %multiply_add_fusion.2), channel_id=1, source_target_pairs={{0,64},{64,128},{128,192},{192,256},{256,320},{320,384},{384,448},... | collective-permute-start | bytes 98312 | tf_op jit(solution)/shard_map/while/body/eval_jaxpr/ppermute | solution.py:12
  217.0 5.2 %collective-permute-start = (f32[1,64,128]{2,1,0:T(8,128)S(1)}, f32[1,64,128]{2,1,0:T(8,128)S(1)}, u32[]{:S(2)}, u32[]{:S(2)}) collective-permute-start(f32[1,64,128]{2,1,0:T(8,128)S(1)} %multiply_add_fusion.2), channel_id=1, source_target_pairs={{0,64},{64,128},{128,192},{192,256},{256,320},{320,384},{384,448},... | collective-permute-start | bytes 98312 | tf_op jit(solution)/shard_map/while/body/eval_jaxpr/ppermute | solution.py:12
  222.4 17.6 %copy-start.6 = (bf16[64]{0:T(256)(128)(2,1)S(1)}, bf16[64]{0:T(256)(128)(2,1)}, u32[]{:S(2)}) copy-start(bf16[64]{0:T(256)(128)(2,1)} %param.26) | copy-start | bytes 388
  227.8 159.8 %all-to-all-start = ((bf16[64,2,1024]{2,1,0:T(2,128)(2,1)}), bf16[64,2,1024]{2,1,0:T(2,128)(2,1)S(1)}, u32[]{:S(2)}, u32[]{:S(2)}) async-start(bf16[64,2,1024]{2,1,0:T(2,128)(2,1)} %reshape.305), calls=%async_computation | async-start | bytes 524288 | tf_op jit(solution)/shard_map/all_to_all | solution.py:106
  388.7 5.8 %copy-start.2 = (bf16[1024,4096]{0,1:T(8,128)(2,1)S(1)}, bf16[1024,4096]{0,1:T(8,128)(2,1)}, u32[]{:S(2)}) copy-start(bf16[1024,4096]{0,1:T(8,128)(2,1)} %all-gather.6.cloned.1.call-done) | copy-start | bytes 25165828
Sparse Core Ops, SparseCore 0:
  10.3 149.6 all-gather.3
  226.6 154.3 all-gather.5
where the time goes:
time: 404 us
  waiting for transfers between devices  176 us (44%)
  blocking collectives  147 us (36%)
  starting transfers between devices  25.8 us (6%)
  between operations  16.4 us (4%)
  matrix products  14.6 us (4%)
  other arithmetic  10.6 us (3%)
  local copies, waits for them, and re-layouts  10.1 us (2%)
    all_gather x1, waiting for transfers between devices, body(): piece = lax.all_gather(tokens, 'head', axis=1, tiled=True)  149 us
    unnamed x1, blocking collectives  147 us
    ppermute x8, waiting for transfers between devices, from_behind(): return lax.ppermute(block, axis, route)  26.6 us
    ppermute x8, starting transfers between devices, from_behind(): return lax.ppermute(block, axis, route)  15.4 us
    dot_general x4, matrix products, product(): return jnp.dot(piece, weight, preferred_element_type=jnp.float32)  11.1 us
    all_to_all x1, starting transfers between devices, body(): lax.all_to_all(out_weight, 'head', split_axis=1, concat_axis=0, tiled=True)  10.3 us
  transfers between devices with their start and end apart: 11, of which 9 were waited for; matrix products, arithmetic and copies ran while one was open for 1% of the time, Pallas kernels for 0%

commit v1 on v0

--- a/solution.py
+++ b/solution.py
@@ -103,7 +103,12 @@
         output_y.reshape(tok_rows, inner_width) * jax.nn.silu(z_in.astype(jnp.float32))
     ).astype(jnp.bfloat16)
     head_count = lax.axis_size("head")
-    columns = lax.all_to_all(out_weight, "head", split_axis=1, concat_axis=0, tiled=True)
+    columns = jnp.concatenate(
+        lax.all_to_all(
+            jnp.stack(jnp.split(out_weight, lax.axis_size("head"), axis=1)), "head", 0, 0
+        ),
+        axis=0,
+    )
     gain_row = norm_gain.reshape(1, inner_width)
     section = lax.all_gather(gated, "head", axis=1, tiled=True)
     gain_part = lax.all_gather(gain_row, "head", axis=1, tiled=True)

time: 404 us -> 412 us (1.020)
  local copies, waits for them, and re-layouts: 10.1 us -> 16.6 us
    unnamed x21 -> x147, local copies, waits for them, and re-layouts: 3.76 us -> 9.74 us
  transfers between devices with their start and end apart: 11 -> 11, of which waited for: 9 -> 9; matrix products, arithmetic and copies ran while one was open for 1% -> 3% of each run, Pallas kernels for 0% -> 0%
where the time goes in v1:
time: 412 us; the launch traced here: 411 us
  waiting for transfers between devices  177 us (43%)
  blocking collectives  148 us (36%)
  starting transfers between devices  25.7 us (6%)
  local copies, waits for them, and re-layouts  16.6 us (4%)
  between operations  16.6 us (4%)
  matrix products  14.5 us (4%)
  other arithmetic  10.7 us (3%)
    all_gather x1, waiting for transfers between devices, body(): piece = lax.all_gather(tokens, 'head', axis=1, tiled=True)  149 us
    unnamed x1, blocking collectives  148 us
    ppermute x8, waiting for transfers between devices, from_behind(): return lax.ppermute(block, axis, route)  26.8 us
    ppermute x8, starting transfers between devices, from_behind(): return lax.ppermute(block, axis, route)  15.4 us
    dot_general x4, matrix products, product(): return jnp.dot(piece, weight, preferred_element_type=jnp.float32)  11 us
    all_to_all x1, starting transfers between devices, body(): lax.all_to_all(jnp.stack(jnp.split(out_weight, lax.axis_size('head'), axi...  10.3 us
    unnamed x147, local copies, waits for them, and re-layouts  9.74 us
  transfers between devices with their start and end apart: 11, of which 9 were waited for; matrix products, arithmetic and copies ran while one was open for 3% of the time, Pallas kernels for 0%

profile of v1, /device:TPU:10, one launch (start us, length us, event | category | flops | bytes accessed | tf_op | source)
XLA Modules:
  0.0 411.1 jit_solution(3887858993039383165)
XLA Ops:
  11.0 148.9 %all-gather.4.cloned.1.call-done = bf16[1024,2048]{0,1:T(8,128)(2,1)} async-done(((bf16[1024,32]{0,1:T(8,128)(2,1)}), bf16[1024,2048]{0,1:T(8,128)(2,1)}) %all-gather.4.cloned.1.call-update) | async-done | bytes 4194320 | tf_op jit(solution)/shard_map/all_gather | solution.py:42
  160.0 2.8 fusion.49
  164.5 3.6 convolution_convert_fusion
  169.2 1.9 collective-permute-start.1
  171.3 3.7 collective-permute-done.1
  176.8 8.1 %while.28 = (s32[]{:T(128)}, f32[1,64,128]{2,1,0:T(8,128)S(1)}, f32[1]{0:T(128)}, f32[4,1,64,128]{3,2,1,0:T(8,128)S(1)}, f32[4,1]{0,1:T(1,128)S(1)}, /*index=5*/...) while((s32[]{:T(128)}, f32[1,64,128]{2,1,0:T(8,128)S(1)}, f32[1]{0:T(128)}, ...), condition=%wide.region_3.4_spmd.clone, body=%wide.region_2.3_spmd.clone.sunk | while | flops 32772 | bytes 164000 | solution.py:87
  185.7 36.8 %while.27 = (s32[]{:T(128)}, f32[1,64,128]{2,1,0:T(8,128)S(1)}, f32[1]{0:T(128)}, f32[1,64,128]{2,1,0:T(8,128)S(1)}, s32[]{:T(128)}) while((s32[]{:T(128)}, f32[1,64,128]{2,1,0:T(8,128)S(1)}, f32[1]{0:T(128)}, f32[1,64,128]{2,1,0:T(8,128)S(1)}, s32[]{:T(128)}) %tuple.113), condition=%wide.region_5.6_spmd, body=%wide.region_4.5_spmd.sunk | while | flops 16386 | bytes 229481 | solution.py:94
  185.7 2.1 collective-permute-start
  187.8 3.3 collective-permute-done
  191.1 1.9 collective-permute-start
  193.0 3.3 collective-permute-done
  196.3 1.9 collective-permute-start
  198.3 3.3 collective-permute-done
  201.6 1.9 collective-permute-start
  203.5 3.3 collective-permute-done
  206.8 1.9 collective-permute-start
  208.7 3.3 collective-permute-done
  214.0 3.3 collective-permute-done
  219.2 3.3 collective-permute-done
  223.0 3.7 multiply_convert_fusion.1
  234.9 10.3 %all-to-all-start = ((bf16[64,2,1024]{2,1,0:T(2,128)(2,1)}), bf16[64,2,1024]{2,1,0:T(2,128)(2,1)S(1)}, u32[]{:S(2)}, u32[]{:S(2)}) async-start(bf16[64,2,1024]{2,1,0:T(2,128)(2,1)} %reshape.306), calls=%async_computation | async-start | bytes 524288 | tf_op jit(solution)/shard_map/all_to_all | solution.py:107
  247.3 147.6 %all-reduce = bf16[4096]{0:T(1024)(128)(2,1)S(1)} all-reduce(bf16[4096]{0:T(1024)(128)(2,1)S(1)} %dynamic-update-slice), channel_id=2, replica_groups=mesh['seq'=8,'head'=64] {'head'}, use_global_device_ids=true, to_apply=%add | all-reduce | flops 4096 | bytes 16384
  396.0 5.2 %fusion.1 = f32[1024]{0:T(1024)S(1)} fusion(bf16[1024,4096]{0,1:T(8,128)(2,1)} %all-gather.6.cloned.1.call-done), kind=kLoop, calls=%fused_computation.7 | loop fusion | flops 12581888 | bytes 8392704 | tf_op jit(solution)/shard_map/reduce_sum | solution.py:118
  401.7 2.5 fusion.17
  (223 shorter events, 28.5 us)
Async XLA Ops:
  6.5 158.0 %copy-start = (bf16[2048,256]{1,0:T(8,128)(2,1)S(1)}, bf16[2048,256]{1,0:T(8,128)(2,1)}, u32[]{:S(2)}) copy-start(bf16[2048,256]{1,0:T(8,128)(2,1)} %param.19) | copy-start | bytes 3145732
  6.5 153.4 %all-gather.4.cloned.1.call-start = ((), (), s32[]{:S(2)}) async-start(), calls=%async_computation.1 | async-start | bytes 4259840 | tf_op jit(solution)/shard_map/all_gather | solution.py:42
  7.3 388.7 %all-gather.6.cloned.1.call-start = ((), (), s32[]{:S(2)}) async-start(), calls=%async_computation.2 | async-start | bytes 8519680 | tf_op jit(solution)/shard_map/all_gather | solution.py:113
  164.5 3.8 copy-start.1
  164.5 3.8 copy-start.4
  169.2 5.8 %collective-permute-start.1 = (bf16[3,320]{0,1:T(8,128)(2,1)S(1)}, bf16[3,320]{0,1:T(8,128)(2,1)S(1)}, u32[]{:S(2)}, u32[]{:S(2)}) collective-permute-start(bf16[3,320]{0,1:T(8,128)(2,1)S(1)} %pad_maximum_fusion.2), channel_id=1, source_target_pairs={{0,64},{64,128},{128,192},{192,256},{256,320},{320,384},{384,448},... | collective-permute-start | bytes 5768 | tf_op jit(solution)/shard_map/ppermute | solution.py:12
  176.6 46.4 %copy-start.5 = (bf16[2048,64]{0,1:T(8,128)(2,1)S(1)}, bf16[2048,64]{0,1:T(8,128)(2,1)}, u32[]{:S(2)}) copy-start(bf16[2048,64]{0,1:T(8,128)(2,1)} %param.17) | copy-start | bytes 786436
  185.7 41.0 %copy-start.3 = (bf16[64,2048]{1,0:T(8,128)(2,1)S(1)}, bf16[64,2048]{1,0:T(8,128)(2,1)}, u32[]{:S(2)}) copy-start(bf16[64,2048]{1,0:T(8,128)(2,1)} %param.27) | copy-start | bytes 786436
  185.7 5.4 %collective-permute-start = (f32[1,64,128]{2,1,0:T(8,128)S(1)}, f32[1,64,128]{2,1,0:T(8,128)S(1)}, u32[]{:S(2)}, u32[]{:S(2)}) collective-permute-start(f32[1,64,128]{2,1,0:T(8,128)S(1)} %multiply_add_fusion.2), channel_id=1, source_target_pairs={{0,64},{64,128},{128,192},{192,256},{256,320},{320,384},{384,448},... | collective-permute-start | bytes 98312 | tf_op jit(solution)/shard_map/while/body/eval_jaxpr/ppermute | solution.py:12
  191.1 5.2 %collective-permute-start = (f32[1,64,128]{2,1,0:T(8,128)S(1)}, f32[1,64,128]{2,1,0:T(8,128)S(1)}, u32[]{:S(2)}, u32[]{:S(2)}) collective-permute-start(f32[1,64,128]{2,1,0:T(8,128)S(1)} %multiply_add_fusion.2), channel_id=1, source_target_pairs={{0,64},{64,128},{128,192},{192,256},{256,320},{320,384},{384,448},... | collective-permute-start | bytes 98312 | tf_op jit(solution)/shard_map/while/body/eval_jaxpr/ppermute | solution.py:12
  196.3 5.2 %collective-permute-start = (f32[1,64,128]{2,1,0:T(8,128)S(1)}, f32[1,64,128]{2,1,0:T(8,128)S(1)}, u32[]{:S(2)}, u32[]{:S(2)}) collective-permute-start(f32[1,64,128]{2,1,0:T(8,128)S(1)} %multiply_add_fusion.2), channel_id=1, source_target_pairs={{0,64},{64,128},{128,192},{192,256},{256,320},{320,384},{384,448},... | collective-permute-start | bytes 98312 | tf_op jit(solution)/shard_map/while/body/eval_jaxpr/ppermute | solution.py:12
  201.6 5.2 %collective-permute-start = (f32[1,64,128]{2,1,0:T(8,128)S(1)}, f32[1,64,128]{2,1,0:T(8,128)S(1)}, u32[]{:S(2)}, u32[]{:S(2)}) collective-permute-start(f32[1,64,128]{2,1,0:T(8,128)S(1)} %multiply_add_fusion.2), channel_id=1, source_target_pairs={{0,64},{64,128},{128,192},{192,256},{256,320},{320,384},{384,448},... | collective-permute-start | bytes 98312 | tf_op jit(solution)/shard_map/while/body/eval_jaxpr/ppermute | solution.py:12
  206.8 5.2 %collective-permute-start = (f32[1,64,128]{2,1,0:T(8,128)S(1)}, f32[1,64,128]{2,1,0:T(8,128)S(1)}, u32[]{:S(2)}, u32[]{:S(2)}) collective-permute-start(f32[1,64,128]{2,1,0:T(8,128)S(1)} %multiply_add_fusion.2), channel_id=1, source_target_pairs={{0,64},{64,128},{128,192},{192,256},{256,320},{320,384},{384,448},... | collective-permute-start | bytes 98312 | tf_op jit(solution)/shard_map/while/body/eval_jaxpr/ppermute | solution.py:12
  212.0 5.2 %collective-permute-start = (f32[1,64,128]{2,1,0:T(8,128)S(1)}, f32[1,64,128]{2,1,0:T(8,128)S(1)}, u32[]{:S(2)}, u32[]{:S(2)}) collective-permute-start(f32[1,64,128]{2,1,0:T(8,128)S(1)} %multiply_add_fusion.2), channel_id=1, source_target_pairs={{0,64},{64,128},{128,192},{192,256},{256,320},{320,384},{384,448},... | collective-permute-start | bytes 98312 | tf_op jit(solution)/shard_map/while/body/eval_jaxpr/ppermute | solution.py:12
  217.3 5.2 %collective-permute-start = (f32[1,64,128]{2,1,0:T(8,128)S(1)}, f32[1,64,128]{2,1,0:T(8,128)S(1)}, u32[]{:S(2)}, u32[]{:S(2)}) collective-permute-start(f32[1,64,128]{2,1,0:T(8,128)S(1)} %multiply_add_fusion.2), channel_id=1, source_target_pairs={{0,64},{64,128},{128,192},{192,256},{256,320},{320,384},{384,448},... | collective-permute-start | bytes 98312 | tf_op jit(solution)/shard_map/while/body/eval_jaxpr/ppermute | solution.py:12
  226.7 20.4 %copy-start.6 = (bf16[64]{0:T(256)(128)(2,1)S(1)}, bf16[64]{0:T(256)(128)(2,1)}, u32[]{:S(2)}) copy-start(bf16[64]{0:T(256)(128)(2,1)} %param.26) | copy-start | bytes 388
  234.9 160.1 %all-to-all-start = ((bf16[64,2,1024]{2,1,0:T(2,128)(2,1)}), bf16[64,2,1024]{2,1,0:T(2,128)(2,1)S(1)}, u32[]{:S(2)}, u32[]{:S(2)}) async-start(bf16[64,2,1024]{2,1,0:T(2,128)(2,1)} %reshape.306), calls=%async_computation | async-start | bytes 524288 | tf_op jit(solution)/shard_map/all_to_all | solution.py:107
  396.0 5.8 %copy-start.2 = (bf16[1024,4096]{0,1:T(8,128)(2,1)S(1)}, bf16[1024,4096]{0,1:T(8,128)(2,1)}, u32[]{:S(2)}) copy-start(bf16[1024,4096]{0,1:T(8,128)(2,1)} %all-gather.6.cloned.1.call-done) | copy-start | bytes 25165828
Sparse Core Ops, SparseCore 0:
  10.3 149.6 all-gather.3
  226.9 155.2 all-gather.5
